TPU v7x, 32 devices: a whole 2x2x4 slice. The times are simulated.
32 devices in a mesh: replica: 4 (over z), fsdp: 2 (over y), tensor: 4 (over x, core).
Axes of the slice: x: 2, y: 2, z: 4, core: 2. Of those that a mesh axis runs over, the one named last changes fastest.
Arguments:
- activations: bfloat16 [1024, 8192], P(('replica', 'fsdp')), may hold values from -6 to 6
- value_grads: bfloat16 [1024, 2048], P(('replica', 'fsdp'), 'tensor'), may hold values from -6 to 6
- lengths: int32 [16], P(('replica', 'fsdp')), may hold values from 16 to 64, as said below
- master: float32 [8192, 2048], P('fsdp', 'tensor'), may hold values from -0.0625 to 0.0625
- moment_one: float32 [8192, 2048], P('fsdp', 'tensor'), may hold values from -0.078125 to 0.078125
- moment_two: float32 [8192, 2048], P('fsdp', 'tensor'), may hold values from 1e-06 to 0.0001
Outputs:
- input_grads: bfloat16 [1024, 8192], P(('replica', 'fsdp'), 'tensor')
- new_master: float32 [8192, 2048], P('fsdp', 'tensor')
- new_moment_one: float32 [8192, 2048], P('fsdp', 'tensor')
- new_moment_two: float32 [8192, 2048], P('fsdp', 'tensor')
Inputs may be any that keep to these rules, and one draw needn't show every extreme that they name: `lengths`: each sequence's live tokens form a prefix of its 64 positions.
All inputs are finite; a program needn't handle non-finite values.
Results may differ from a plain program's by a relative error of at most 0.014.
Values may be sent and summed in bfloat16 or wider, within the bound.
A program may use at most 128 MiB of HBM per device.

v0:
```python
import jax
import jax.numpy as jnp
from jax import lax
from jax.sharding import PartitionSpec as P

beta_one = 0.9
beta_two = 0.95
learn_rate = 0.001
weight_decay = 0.1
adam_step = 10
epsilon = 1e-08


def adamw(grad, master, moment_one, moment_two):
    first = beta_one * moment_one + (1.0 - beta_one) * grad
    second = beta_two * moment_two + (1.0 - beta_two) * grad * grad
    first_hat = first / (1.0 - beta_one**adam_step)
    second_hat = second / (1.0 - beta_two**adam_step)
    updated = master - learn_rate * (
        first_hat / (jnp.sqrt(second_hat) + epsilon) + weight_decay * master
    )
    return (updated, first, second)


def local(activations, value_grads, lengths, master, moment_one, moment_two):
    tok_rows = activations.shape[0]
    seq_count = lengths.shape[0]
    seq_len = tok_rows // seq_count
    index = jnp.arange(tok_rows, dtype=jnp.int32)
    owner = index // seq_len
    pick = owner[:, None] == jnp.arange(seq_count, dtype=jnp.int32)[None, :]
    limit = jnp.sum(jnp.where(pick, lengths[None, :], 0), axis=1)
    masked = jnp.where((index % seq_len < limit)[:, None], value_grads, jnp.zeros_like(value_grads))
    weight = master.astype(jnp.bfloat16)
    terms = lax.dot_general(
        masked,
        lax.all_gather(weight, "fsdp", axis=0, tiled=True),
        (((1,), (1,)), ((), ())),
        preferred_element_type=jnp.float32,
    )
    input_grads = lax.psum_scatter(
        terms.astype(jnp.bfloat16), "tensor", scatter_dimension=1, tiled=True
    )
    shard_rows = lax.psum_scatter(
        lax.dot_general(
            activations, masked, (((0,), (0,)), ((), ())), preferred_element_type=jnp.float32
        ).astype(jnp.bfloat16),
        "fsdp",
        scatter_dimension=0,
        tiled=True,
    )
    count = float(tok_rows * lax.axis_size("replica") * lax.axis_size("fsdp"))
    summed = lax.psum(shard_rows, "replica").astype(jnp.float32)
    new_master, new_one, new_two = adamw(summed / count, master, moment_one, moment_two)
    return (input_grads, new_master, new_one, new_two)


def solution(mesh):
    in_specs = (
        P(("replica", "fsdp"), None),
        P(("replica", "fsdp"), "tensor"),
        P(("replica", "fsdp")),
        P("fsdp", "tensor"),
        P("fsdp", "tensor"),
        P("fsdp", "tensor"),
    )
    out_specs = (
        P(("replica", "fsdp"), "tensor"),
        P("fsdp", "tensor"),
        P("fsdp", "tensor"),
        P("fsdp", "tensor"),
    )
    return jax.shard_map(local, mesh=mesh, in_specs=in_specs, out_specs=out_specs, check_vma=False)
```

profile of v0, /device:TPU:2, one launch (start us, length us, event | category | flops | bytes accessed | tf_op | source)
XLA Modules:
  0.0 434.6 jit_solution(12900411031065450978)
XLA Ops:
  7.2 0.0 copy-start
  7.2 0.0 reduce-scatter.5.cloned.1.call-start
  7.2 0.9 fusion.4
  8.1 0.7 copy-done
  8.8 6.7 %fusion = bf16[8192,512]{0,1:T(8,128)(2,1)} fusion(bf16[128,8192]{1,0:T(8,128)(2,1)S(1)} %copy-done, bf16[128,512]{1,0:T(8,128)(2,1)} %param.7, pred[128]{0:T(512)(128)(4,1)S(1)} %fusion.5), kind=kOutput, calls=%fused_computation.4 | convolution fusion | flops 1078001664 | bytes 10616960 | tf_op jit(solution)/shard_map/dot_general | solution.py:45
  15.5 0.0 reduce-scatter.5.cloned.1.call-update
  15.6 0.0 all-gather.2.cloned.1.call-start
  15.6 5.9 %convert_element_type.15 = bf16[4096,512]{1,0:T(8,128)(2,1)} convert(f32[4096,512]{1,0:T(8,128)} %param.9) | non-fusion elementwise | flops 2097152 | bytes 12582912 | tf_op jit(solution)/shard_map/convert_element_type | solution.py:34
  21.5 0.0 all-gather.2.cloned.1.call-update
  21.6 0.0 all-reduce.2.cloned.1.call-start
  21.6 94.6 %reduce-scatter.5.cloned.1.call-done = bf16[4096,512]{0,1:T(8,128)(2,1)} async-done(((bf16[8192,512]{0,1:T(8,128)(2,1)}), bf16[4096,512]{0,1:T(8,128)(2,1)}) %reduce-scatter.5.cloned.1.call-update) | async-done | bytes 4194320 | tf_op jit(solution)/shard_map/reduce_scatter | solution.py:44
  116.2 0.0 all-reduce.2.cloned.1.call-update
  116.2 0.0 reduce-scatter.3.cloned.1.call-start
  116.2 106.2 %all-gather.2.cloned.1.call-done = bf16[8192,512]{1,0:T(8,128)(2,1)} async-done(((bf16[4096,512]{1,0:T(8,128)(2,1)}), bf16[8192,512]{1,0:T(8,128)(2,1)}) %all-gather.2.cloned.1.call-update) | async-done | bytes 8388624 | tf_op jit(solution)/shard_map/all_gather | solution.py:37
  222.4 7.5 %convolution_convert_fusion.1 = bf16[128,8192]{1,0:T(8,128)(2,1)} fusion(bf16[8192,512]{1,0:T(8,128)(2,1)} %all-gather.2.cloned.1.call-done, bf16[128,512]{1,0:T(8,128)(2,1)S(1)} %copy-done.2, pred[128]{0:T(512)(128)(4,1)S(1)} %fusion.5), kind=kOutput, calls=%fused_computation.5 | convolution fusion | flops 1074855936 | bytes 10616960 | tf_op jit(solution)/shard_map/dot_general | solution.py:35
  230.0 0.0 reduce-scatter.3.cloned.1.call-update
  230.0 9.4 %copy.20 = f32[4096,512]{0,1:T(8,128)} copy(f32[4096,512]{1,0:T(8,128)} %param.9) | data formatting | bytes 16777216 | tf_op args[3]
  239.3 8.9 %copy.17 = f32[4096,512]{0,1:T(8,128)} copy(f32[4096,512]{1,0:T(8,128)} %param.10) | data formatting | bytes 16777216 | tf_op args[4]
  248.2 8.9 %copy.18 = f32[4096,512]{0,1:T(8,128)} copy(f32[4096,512]{1,0:T(8,128)} %param.11) | data formatting | bytes 16777216 | tf_op args[5]
  257.2 122.8 %all-reduce.2.cloned.1.call-done = bf16[4096,512]{0,1:T(8,128)(2,1)} async-done(((bf16[4096,512]{0,1:T(8,128)(2,1)}), bf16[4096,512]{0,1:T(8,128)(2,1)}) %all-reduce.2.cloned.1.call-update) | async-done | bytes 4194320 | tf_op jit(solution)/shard_map/psum | solution.py:53
  380.0 21.1 %multiply_subtract_fusion = (f32[4096,512]{0,1:T(8,128)}, f32[4096,512]{0,1:T(8,128)}, f32[4096,512]{0,1:T(8,128)}) fusion(f32[4096,512]{0,1:T(8,128)} %copy.20, bf16[4096,512]{0,1:T(8,128)(2,1)} %all-reduce.2.cloned.1.call-done, f32[4096,512]{0,1:T(8,128)} %copy.17, f32[4096,512]{0,1:T(8,128)} %copy.18), kind=kLoop, calls=%fused_computation.9 | loop fusion | flops 35651584 | bytes 54525952 | tf_op jit(solution)/shard_map/sub | solution.py:19
  401.1 8.9 %copy.21 = f32[4096,512]{1,0:T(8,128)} copy(f32[4096,512]{0,1:T(8,128)} %get-tuple-element.12) | data formatting | bytes 16777216
  410.1 8.9 %copy.22 = f32[4096,512]{1,0:T(8,128)} copy(f32[4096,512]{0,1:T(8,128)} %get-tuple-element.13) | data formatting | bytes 16777216
  419.0 9.1 %copy.23 = f32[4096,512]{1,0:T(8,128)} copy(f32[4096,512]{0,1:T(8,128)} %get-tuple-element.14) | data formatting | bytes 16777216
  (7 shorter events, 0.0 us)
Async XLA Ops:
  7.2 1.6 copy-start
  7.2 109.0 %reduce-scatter.5.cloned.1.call-start = ((), (), s32[]{:S(2)}) async-start(), calls=%async_computation.4 | async-start | bytes 12582912 | tf_op jit(solution)/shard_map/reduce_scatter | solution.py:44
  15.5 206.9 %copy-start.2 = (bf16[128,512]{1,0:T(8,128)(2,1)S(1)}, bf16[128,512]{1,0:T(8,128)(2,1)}, u32[]{:S(2)}) copy-start(bf16[128,512]{1,0:T(8,128)(2,1)} %param.7) | copy-start | bytes 393220
  15.6 206.9 %all-gather.2.cloned.1.call-start = ((), (), s32[]{:S(2)}) async-start(), calls=%async_computation.2 | async-start | bytes 12582912 | tf_op jit(solution)/shard_map/all_gather | solution.py:37
  21.6 358.4 %all-reduce.2.cloned.1.call-start = ((), (), s32[]{:S(2)}) async-start(), calls=%async_computation.5 | async-start | bytes 8388608 | tf_op jit(solution)/shard_map/psum | solution.py:53
  116.2 311.9 %reduce-scatter.3.cloned.1.call-start = ((), (), s32[]{:S(2)}) async-start(), calls=%async_computation.3 | async-start | bytes 2621440 | tf_op jit(solution)/shard_map/reduce_scatter | solution.py:41
  419.0 9.1 %copy-start.1 = (bf16[128,8192]{1,0:T(8,128)(2,1)S(1)}, bf16[128,8192]{1,0:T(8,128)(2,1)}, u32[]{:S(2)}) copy-start(bf16[128,8192]{1,0:T(8,128)(2,1)} %param.6) | copy-start | bytes 6291460
Sparse Core Ops, SparseCore 0:
  15.7 100.4 reduce-scatter.4
  118.4 103.9 all-gather.1
  224.9 155.0 all-reduce.1
  382.9 29.2 reduce-scatter.2
where the time goes:
time: 437 us; the launch traced here: 435 us
  waiting for transfers between devices  324 us (74%)
  local copies, waits for them, and re-layouts  54.8 us (13%)
  other arithmetic  28 us (6%)
  matrix products  14.3 us (3%)
  between operations  13.8 us (3%)
    psum x1, waiting for transfers between devices, local(): summed = lax.psum(shard_rows, 'replica').astype(jnp.float32)  123 us
    all_gather x1, waiting for transfers between devices, local(): lax.all_gather(weight, 'fsdp', axis=0, tiled=True)  106 us
    reduce_scatter x1, waiting for transfers between devices, local(): lax.psum_scatter(lax.dot_general(activations, masked, (((0,), (0,)), ((),...  94.6 us
    unnamed x12, local copies, waits for them, and re-layouts  54.8 us
    sub x1, other arithmetic, adamw(): master - learn_rate * (first_hat / (jnp.sqrt(second_hat) + epsilon) + wei...  21.1 us
  transfers between devices with their start and end apart: 4, of which 3 were waited for; matrix products, arithmetic and copies ran while one was open for 20% of the time, Pallas kernels for 0%

commit v1 on v0

--- a/solution.py
+++ b/solution.py
@@ -1,7 +1,14 @@
+import functools
+
 import jax
 import jax.numpy as jnp
 from jax import lax
+from jax.experimental import pallas as pl
+from jax.experimental.pallas import tpu as pltpu
 from jax.sharding import PartitionSpec as P
+
+MESH = pl.DeviceIdType.MESH
+LANE = 128
 
 beta_one = 0.9
 beta_two = 0.95
@@ -55,6 +62,345 @@
     return (input_grads, new_master, new_one, new_two)
 
 
+def exchange(R, T, H, K, lens, acts, grads_in, master, ig_out, grad_out, G, M, W, part, core_in,
+             y_in, x_in, l_sem, w_sem, ys, yr, zs, zr, xs, xr, cs, cr, mzs, mzr, mys, myr, igs, igr):
+    r, f, t = lax.axis_index("replica"), lax.axis_index("fsdp"), lax.axis_index("tensor")
+    x, c = t // 2, t % 2
+    other_f, sib, across = 1 - f, 2 * x + 1 - c, 2 * (1 - x) + c
+    width = 4 * LANE
+    half = H // 2
+
+    def dev(replica=r, fsdp=f, tensor=t):
+        return {"replica": replica, "fsdp": fsdp, "tensor": tensor}
+
+    def remote(src, dst, send, recv, to):
+        return pltpu.make_async_remote_copy(
+            src_ref=src, dst_ref=dst, send_sem=send, recv_sem=recv, device_id=to, device_id_type=MESH
+        )
+
+    def rows(o, ff):
+        return pl.ds(pl.multiple_of((2 * o + ff) * T, T), T)
+
+    def plane(o):
+        return pl.ds(pl.multiple_of(2 * o * T, T), 2 * T)
+
+    def lanes(q):
+        return pl.ds(pl.multiple_of(q * LANE, LANE), LANE)
+
+    def columns(ff, k, q):
+        return pl.ds(pl.multiple_of(ff * H + k * width + q * LANE, LANE), LANE)
+
+    def own_copy(k, j, q):
+        return pltpu.make_async_copy(
+            acts.at[:, columns(f, k, q)], G.at[k, rows(r, f), lanes(q)], l_sem.at[k, j]
+        )
+
+    def y_copy(k, j, q):
+        return remote(
+            acts.at[:, columns(other_f, k, q)], G.at[k, rows(r, f), lanes(q)],
+            ys.at[k, j], yr.at[k, j], dev(fsdp=other_f),
+        )
+
+    def z_copy(k, o, way, to):
+        ref = G.at[k, plane(o), lanes(t)]
+        return remote(ref, ref, zs.at[k, o, way], zr.at[k, o], dev(replica=to))
+
+    def x_copy(k, o, q):
+        ref = G.at[k, plane(o), lanes(q)]
+        return remote(ref, ref, xs.at[k, o], xr.at[k, o], dev(tensor=across))
+
+    def c_copy(k, j, q):
+        ref = G.at[k, :, lanes(q)]
+        return remote(ref, ref, cs.at[k, j], cr.at[k, j], dev(tensor=sib))
+
+    def mz_copy(o, way, to):
+        ref = M.at[rows(o, f)]
+        return remote(ref, ref, mzs.at[o, way], mzr.at[o], dev(replica=to))
+
+    def my_copy(o, ff):
+        ref = M.at[rows(o, ff)]
+        return remote(ref, ref, mys.at[o], myr.at[o], dev(fsdp=other_f))
+
+    piece = pl.ds(pl.multiple_of(f * T, T), T)
+    other_piece = pl.ds(pl.multiple_of(other_f * T, T), T)
+    ig_core = remote(part.at[0], core_in, igs.at[0], igr.at[0], dev(tensor=sib))
+    ig_y = remote(part.at[1, other_piece], y_in, igs.at[1], igr.at[1], dev(fsdp=other_f))
+    ig_x_own = remote(part.at[1, piece], x_in, igs.at[2], igr.at[2], dev(tensor=across))
+    ig_x_relay = remote(y_in, x_in, igs.at[2], igr.at[2], dev(tensor=across))
+    on = x == f
+
+    def w_copy(j, cc):
+        ref = pl.ds(pl.multiple_of(cc * half, half), half)
+        return pltpu.make_async_copy(master.at[ref], W.at[ref], w_sem.at[j])
+
+    w_copy(0, 1 - c).start()
+    w_copy(1, c).start()
+
+    def start_own(k):
+        own_copy(k, 0, t).start()
+        own_copy(k, 1, across).start()
+
+    def start_y(k):
+        y_copy(k, 0, t).start()
+        y_copy(k, 1, across).start()
+
+    @pl.loop(0, K)
+    def _(k):
+        start_own(k)
+
+    seqs = lens.shape[0]
+    seq = T // seqs
+    for j in range(seqs):
+        at = lax.broadcasted_iota(jnp.int32, (seq, grads_in.shape[1]), 0)
+        value = grads_in[j * seq:(j + 1) * seq, :].astype(jnp.float32)
+        value = jnp.where(at < lens[j], value, jnp.zeros_like(value))
+        M[pl.ds(pl.multiple_of((2 * r + f) * T + j * seq, seq), seq), :] = value.astype(jnp.bfloat16)
+
+    barrier = pltpu.get_barrier_semaphore()
+    for to in (dev(fsdp=other_f), dev(tensor=sib), dev(tensor=across)):
+        pl.semaphore_signal(barrier, inc=1, device_id=to, device_id_type=MESH)
+
+    @pl.when(r > 0)
+    def _():
+        pl.semaphore_signal(barrier, inc=1, device_id=dev(replica=r - 1), device_id_type=MESH)
+
+    @pl.when(r < R - 1)
+    def _():
+        pl.semaphore_signal(barrier, inc=1, device_id=dev(replica=r + 1), device_id_type=MESH)
+
+    @pl.when(jnp.logical_or(r == 0, r == R - 1))
+    def _():
+        pl.semaphore_wait(barrier, 4)
+
+    @pl.when(jnp.logical_and(r > 0, r < R - 1))
+    def _():
+        pl.semaphore_wait(barrier, 5)
+
+    my_copy(r, f).start()
+    start_y(0)
+
+    @pl.when(r > 0)
+    def _():
+        mz_copy(r, 1, r - 1).start()
+
+    @pl.when(r < R - 1)
+    def _():
+        mz_copy(r, 0, r + 1).start()
+
+    def from_left(d, extra, body):
+        @pl.when(jnp.logical_and(r >= d, extra))
+        def _():
+            body(r - d)
+
+    def from_right(d, extra, body):
+        @pl.when(jnp.logical_and(r + d < R, extra))
+        def _():
+            body(r + d)
+
+    def pass_on(start, way):
+        @pl.when(r < R - 1 if way == 0 else r > 0)
+        def _():
+            start(r + 1 if way == 0 else r - 1)
+
+    def weight_terms(slot, cc):
+        @pl.loop(0, half // width)
+        def _(i):
+            w = W[pl.ds(pl.multiple_of(cc * half + i * width, width), width), :].astype(jnp.bfloat16)
+            product = lax.dot_general(
+                M[plane(r), :], w, (((1,), (1,)), ((), ())), preferred_element_type=jnp.float32
+            )
+            part[slot, :, pl.ds(pl.multiple_of(i * width, width), width)] = product.astype(jnp.bfloat16)
+
+    @pl.loop(0, K + R + 1)
+    def _(s):
+        @pl.when(s + 1 < K)
+        def _():
+            start_y(s + 1)
+
+        for d in range(R - 1, 0, -1):
+            k = s - d
+            for side, way in ((from_left, 0), (from_right, 1)):
+                def arrived(o, k=k, way=way):
+                    z_copy(k, o, way, o).wait_recv()
+                    pass_on(lambda to: z_copy(k, o, way, to).start(), way)
+                    x_copy(k, o, t).start()
+
+                side(d, jnp.logical_and(k >= 0, k < K), arrived)
+
+                def masked_arrived(o, way=way):
+                    mz_copy(o, way, o).wait_recv()
+                    pass_on(lambda to: mz_copy(o, way, to).start(), way)
+                    my_copy(o, f).start()
+
+                side(d, s == d, masked_arrived)
+
+        @pl.when(s < K)
+        def _():
+            own_copy(s, 0, t).wait()
+            own_copy(s, 1, across).wait()
+            for j, q in ((0, t), (1, across)):
+                remote(
+                    acts.at[:, columns(f, s, q)], G.at[s, rows(r, other_f), lanes(q)],
+                    ys.at[s, j], yr.at[s, j], dev(fsdp=other_f),
+                ).wait_recv()
+            for way in (0, 1):
+                pass_on(lambda to, way=way: z_copy(s, r, way, to).start(), way)
+
+        for d in range(R - 1, 0, -1):
+            k = s - d - 1
+            for side in (from_left, from_right):
+                side(d, jnp.logical_and(k >= 0, k < K),
+                     lambda o, k=k: x_copy(k, o, across).wait_recv())
+
+        full = s - (R - 1)
+
+        @pl.when(jnp.logical_and(full >= 0, full < K))
+        def _():
+            c_copy(full, 0, t).start()
+
+        @pl.when(jnp.logical_and(full >= 1, full <= K))
+        def _():
+            c_copy(full - 1, 1, across).start()
+
+        @pl.when(s == 1)
+        def _():
+            my_copy(r, other_f).wait_recv()
+            w_copy(0, 1 - c).wait()
+            weight_terms(0, 1 - c)
+            ig_core.start()
+            w_copy(1, c).wait()
+            weight_terms(1, c)
+
+        @pl.when(s == 2)
+        def _():
+            ig_core.wait_recv()
+
+            @pl.loop(0, 2 * T // 32)
+            def _(i):
+                at = pl.ds(pl.multiple_of(i * 32, 32), 32)
+                total = part[1, at, :].astype(jnp.float32) + core_in[at, :].astype(jnp.float32)
+                part[1, at, :] = total.astype(jnp.bfloat16)
+
+            ig_y.start()
+
+            @pl.when(jnp.logical_not(on))
+            def _():
+                ig_x_own.start()
+
+        @pl.when(s == 4)
+        def _():
+            ig_y.wait_recv()
+
+            @pl.when(on)
+            def _():
+                ig_x_relay.start()
+
+        @pl.when(s == R + 1)
+        def _():
+            for d in range(1, R):
+                for side in (from_left, from_right):
+                    side(d, True, lambda o: my_copy(o, other_f).wait_recv())
+
+        done = s - R - 1 + 0
+
+        @pl.when(done >= 0)
+        def _():
+            c_copy(done, 0, sib).wait_recv()
+            c_copy(done, 1, 3 - t).wait_recv()
+            product = lax.dot_general(
+                G[done], M[...], (((0,), (0,)), ((), ())), preferred_element_type=jnp.float32
+            )
+            grad_out[pl.ds(pl.multiple_of(done * width, width), width), :] = product.astype(jnp.bfloat16)
+
+    ig_x_own.wait_recv()
+
+    @pl.loop(0, T // 32)
+    def _(i):
+        at = pl.ds(pl.multiple_of(i * 32, 32), 32)
+        mine = part[1, pl.ds(pl.multiple_of(f * T + i * 32, 32), 32), :].astype(jnp.float32)
+        near = jnp.where(on, mine, y_in[at, :].astype(jnp.float32))
+        ig_out[at, :] = (near + x_in[at, :].astype(jnp.float32)).astype(jnp.bfloat16)
+
+    @pl.loop(0, K)
+    def _(k):
+        for j in (0, 1):
+            y_copy(k, j, t).wait_send()
+            c_copy(k, j, t).wait_send()
+        for way in (0, 1):
+            pass_on(lambda to, way=way: z_copy(k, r, way, to).wait_send(), way)
+        for d in range(1, R):
+            for side, way in ((from_left, 0), (from_right, 1)):
+                def drain(o, way=way):
+                    pass_on(lambda to: z_copy(k, o, way, to).wait_send(), way)
+                    x_copy(k, o, t).wait_send()
+
+                side(d, True, drain)
+
+    my_copy(r, f).wait_send()
+    for way in (0, 1):
+        pass_on(lambda to, way=way: mz_copy(r, way, to).wait_send(), way)
+    for d in range(1, R):
+        for side, way in ((from_left, 0), (from_right, 1)):
+            def drain_masked(o, way=way):
+                pass_on(lambda to: mz_copy(o, way, to).wait_send(), way)
+                my_copy(o, f).wait_send()
+
+            side(d, True, drain_masked)
+    ig_core.wait_send()
+    ig_y.wait_send()
+    ig_x_own.wait_send()
+
+
+def local_fast(R, activations, value_grads, lengths, master, moment_one, moment_two):
+    T, D = activations.shape
+    H, V = master.shape
+    K = H // (4 * LANE)
+    half = H // 2
+    dma = pltpu.SemaphoreType.DMA
+    input_grads, grad_sum = pl.pallas_call(
+        functools.partial(exchange, R, T, H, K),
+        out_shape=(
+            jax.ShapeDtypeStruct((T, half), jnp.bfloat16),
+            jax.ShapeDtypeStruct((H, V), jnp.bfloat16),
+        ),
+        in_specs=[
+            pl.BlockSpec(memory_space=pltpu.SMEM),
+            pl.BlockSpec(memory_space=pl.ANY),
+            pl.BlockSpec(memory_space=pltpu.VMEM),
+            pl.BlockSpec(memory_space=pl.ANY),
+        ],
+        out_specs=(pl.BlockSpec(memory_space=pltpu.VMEM), pl.BlockSpec(memory_space=pltpu.VMEM)),
+        scratch_shapes=[
+            pltpu.VMEM((K, 2 * R * T, 4 * LANE), jnp.bfloat16),
+            pltpu.VMEM((2 * R * T, V), jnp.bfloat16),
+            pltpu.VMEM((H, V), jnp.float32),
+            pltpu.VMEM((2, 2 * T, half), jnp.bfloat16),
+            pltpu.VMEM((2 * T, half), jnp.bfloat16),
+            pltpu.VMEM((T, half), jnp.bfloat16),
+            pltpu.VMEM((T, half), jnp.bfloat16),
+            dma((K, 2)), dma((2,)),
+            dma((K, 2)), dma((K, 2)),
+            dma((K, R, 2)), dma((K, R)),
+            dma((K, R)), dma((K, R)),
+            dma((K, 2)), dma((K, 2)),
+            dma((R, 2)), dma((R,)),
+            dma((R,)), dma((R,)),
+            dma((3,)), dma((3,)),
+        ],
+        compiler_params=pltpu.CompilerParams(
+            collective_id=0, has_side_effects=True, vmem_limit_bytes=32 * 1024 * 1024
+        ),
+        cost_estimate=pl.CostEstimate(
+            flops=2 * 2 * R * T * H * V, bytes_accessed=20 * 1024 * 1024, transcendentals=0
+        ),
+    )(lengths, activations, value_grads, master)
+    count = float(T * lax.axis_size("replica") * lax.axis_size("fsdp"))
+    new_master, new_one, new_two = adamw(
+        grad_sum.astype(jnp.float32) / count, master, moment_one, moment_two
+    )
+    return (input_grads, new_master, new_one, new_two)
+
+
 def solution(mesh):
     in_specs = (
         P(("replica", "fsdp"), None),
@@ -70,4 +416,8 @@
         P("fsdp", "tensor"),
         P("fsdp", "tensor"),
     )
-    return jax.shard_map(local, mesh=mesh, in_specs=in_specs, out_specs=out_specs, check_vma=False)
+    shape = mesh.shape
+    body = local
+    if shape["fsdp"] == 2 and shape["tensor"] == 4 and shape["replica"] == 4:
+        body = functools.partial(local_fast, shape["replica"])
+    return jax.shard_map(body, mesh=mesh, in_specs=in_specs, out_specs=out_specs, check_vma=False)

time: 437 us -> 111 us (0.25)
  the two profiles are of different devices: /device:TPU:2 before, /device:TPU:1 now
where the time goes in v1:
time: 111 us; the launch traced here: 110 us
  Pallas kernels  80.2 us (72%)
  other arithmetic  20.4 us (18%)
  local copies, waits for them, and re-layouts  9.26 us (8%)
    pallas_call x1, Pallas kernels, local_fast(): pl.pallas_call(functools.partial(exchange, R, T, H, K), out_shape=(jax.Sh...  80.2 us
    sub x1, other arithmetic, adamw(): master - learn_rate * (first_hat / (jnp.sqrt(second_hat) + epsilon) + wei...  20.4 us
    unnamed x11, local copies, waits for them, and re-layouts  9.26 us

profile of v1, /device:TPU:1, one launch (start us, length us, event | category | flops | bytes accessed | tf_op | source)
XLA Modules:
  0.0 110.5 jit_solution(11260114153346818063)
XLA Ops:
  0.6 0.0 copy-start
  0.6 3.4 %copy-done = f32[4096,512]{1,0:T(8,128)S(1)} copy-done((f32[4096,512]{1,0:T(8,128)S(1)}, f32[4096,512]{1,0:T(8,128)}, u32[]{:S(2)}) %copy-start) | copy-done | bytes 8388632
  4.0 0.0 copy-start.2
  4.0 1.6 %copy-done.2 = bf16[128,8192]{1,0:T(8,128)(2,1)S(1)} copy-done((bf16[128,8192]{1,0:T(8,128)(2,1)S(1)}, bf16[128,8192]{1,0:T(8,128)(2,1)}, u32[]{:S(2)}) %copy-start.2) | copy-done | bytes 2097176
  5.6 0.0 copy-start.3
  5.6 0.9 copy-done.3
  6.5 0.0 copy-start.4
  6.5 0.7 copy-done.4
  7.2 80.2 %shard_map.93 = (bf16[128,2048]{1,0:T(8,128)(2,1)S(1)}, bf16[4096,512]{1,0:T(8,128)(2,1)S(1)}) custom-call(s32[2]{0:T(128)S(1)} %copy-done.4, bf16[128,8192]{1,0:T(8,128)(2,1)S(1)} %copy-done.2, bf16[128,512]{1,0:T(8,128)(2,1)S(1)} %copy-done.3, f32[4096,512]{1,0:T(8,128)S(1)} %copy-done), custom_call_target="tpu_custom_call" | custom-call | flops 4294967296 | bytes 20971520 | tf_op jit(solution)/shard_map/pallas_call | solution.py:360
  87.3 0.0 copy-start.1
  87.3 1.9 %copy-done.1 = bf16[4096,512]{1,0:T(8,128)(2,1)} copy-done((bf16[4096,512]{1,0:T(8,128)(2,1)}, bf16[4096,512]{1,0:T(8,128)(2,1)S(1)}, u32[]{:S(2)}) %copy-start.1) | copy-done | bytes 4194328
  89.3 20.4 %multiply_subtract_fusion = (f32[4096,512]{1,0:T(8,128)}, f32[4096,512]{1,0:T(8,128)}, f32[4096,512]{1,0:T(8,128)}) fusion(f32[4096,512]{1,0:T(8,128)} %master.1, bf16[4096,512]{1,0:T(8,128)(2,1)} %copy-done.1, f32[4096,512]{1,0:T(8,128)} %param.10, f32[4096,512]{1,0:T(8,128)} %param.11), kind=kLoop, calls=%fused_computation.6 | loop fusion | flops 35651584 | bytes 54525952 | tf_op jit(solution)/shard_map/sub | solution.py:26
  109.7 0.8 copy.11
Async XLA Ops:
  0.6 3.4 %copy-start = (f32[4096,512]{1,0:T(8,128)S(1)}, f32[4096,512]{1,0:T(8,128)}, u32[]{:S(2)}) copy-start(f32[4096,512]{1,0:T(8,128)} %master.1) | copy-start | bytes 25165828
  4.0 1.6 %copy-start.2 = (bf16[128,8192]{1,0:T(8,128)(2,1)S(1)}, bf16[128,8192]{1,0:T(8,128)(2,1)}, u32[]{:S(2)}) copy-start(bf16[128,8192]{1,0:T(8,128)(2,1)} %acts.1) | copy-start | bytes 6291460
  5.6 0.9 copy-start.3
  6.5 0.7 copy-start.4
  87.3 1.9 %copy-start.1 = (bf16[4096,512]{1,0:T(8,128)(2,1)}, bf16[4096,512]{1,0:T(8,128)(2,1)S(1)}, u32[]{:S(2)}) copy-start(bf16[4096,512]{1,0:T(8,128)(2,1)S(1)} %get-tuple-element.7) | copy-start | bytes 12582916

commit v2 on v1

--- a/solution.py
+++ b/solution.py
@@ -62,8 +62,8 @@
     return (input_grads, new_master, new_one, new_two)
 
 
-def exchange(R, T, H, K, lens, acts, grads_in, master, ig_out, grad_out, G, M, W, part, core_in,
-             y_in, x_in, l_sem, w_sem, ys, yr, zs, zr, xs, xr, cs, cr, mzs, mzr, mys, myr, igs, igr):
+def exchange(R, T, H, K, lens, acts, grads_in, master, one_in, two_in, ig_out, W, one, two, G, M,
+             own_in, product, part, core_in, y_in, x_in, l_sem, w_sem, ys, yr, zs, zr, xs, xr, cs, cr, mzs, mzr, mys, myr, igs, igr):
     r, f, t = lax.axis_index("replica"), lax.axis_index("fsdp"), lax.axis_index("tensor")
     x, c = t // 2, t % 2
     other_f, sib, across = 1 - f, 2 * x + 1 - c, 2 * (1 - x) + c
@@ -133,8 +133,11 @@
         ref = pl.ds(pl.multiple_of(cc * half, half), half)
         return pltpu.make_async_copy(master.at[ref], W.at[ref], w_sem.at[j])
 
+    grads_copy = pltpu.make_async_copy(grads_in, own_in, w_sem.at[2])
+    one_copy = pltpu.make_async_copy(one_in, one, w_sem.at[3])
+    two_copy = pltpu.make_async_copy(two_in, two, w_sem.at[4])
+    grads_copy.start()
     w_copy(0, 1 - c).start()
-    w_copy(1, c).start()
 
     def start_own(k):
         own_copy(k, 0, t).start()
@@ -148,11 +151,15 @@
     def _(k):
         start_own(k)
 
+    w_copy(1, c).start()
+    one_copy.start()
+    two_copy.start()
+    grads_copy.wait()
     seqs = lens.shape[0]
     seq = T // seqs
     for j in range(seqs):
-        at = lax.broadcasted_iota(jnp.int32, (seq, grads_in.shape[1]), 0)
-        value = grads_in[j * seq:(j + 1) * seq, :].astype(jnp.float32)
+        at = lax.broadcasted_iota(jnp.int32, (seq, own_in.shape[1]), 0)
+        value = own_in[j * seq:(j + 1) * seq, :].astype(jnp.float32)
         value = jnp.where(at < lens[j], value, jnp.zeros_like(value))
         M[pl.ds(pl.multiple_of((2 * r + f) * T + j * seq, seq), seq), :] = value.astype(jnp.bfloat16)
 
@@ -178,6 +185,7 @@
 
     my_copy(r, f).start()
     start_y(0)
+    start_y(1)
 
     @pl.when(r > 0)
     def _():
@@ -213,26 +221,9 @@
 
     @pl.loop(0, K + R + 1)
     def _(s):
-        @pl.when(s + 1 < K)
-        def _():
-            start_y(s + 1)
-
-        for d in range(R - 1, 0, -1):
-            k = s - d
-            for side, way in ((from_left, 0), (from_right, 1)):
-                def arrived(o, k=k, way=way):
-                    z_copy(k, o, way, o).wait_recv()
-                    pass_on(lambda to: z_copy(k, o, way, to).start(), way)
-                    x_copy(k, o, t).start()
-
-                side(d, jnp.logical_and(k >= 0, k < K), arrived)
-
-                def masked_arrived(o, way=way):
-                    mz_copy(o, way, o).wait_recv()
-                    pass_on(lambda to: mz_copy(o, way, to).start(), way)
-                    my_copy(o, f).start()
-
-                side(d, s == d, masked_arrived)
+        @pl.when(s + 2 < K)
+        def _():
+            start_y(s + 2)
 
         @pl.when(s < K)
         def _():
@@ -245,6 +236,22 @@
                 ).wait_recv()
             for way in (0, 1):
                 pass_on(lambda to, way=way: z_copy(s, r, way, to).start(), way)
+        for d in range(R - 1, 0, -1):
+            k = s - d
+            for side, way in ((from_left, 0), (from_right, 1)):
+                def arrived(o, k=k, way=way):
+                    z_copy(k, o, way, o).wait_recv()
+                    pass_on(lambda to: z_copy(k, o, way, to).start(), way)
+                    x_copy(k, o, t).start()
+
+                side(d, jnp.logical_and(k >= 0, k < K), arrived)
+
+                def masked_arrived(o, way=way):
+                    mz_copy(o, way, o).wait_recv()
+                    pass_on(lambda to: mz_copy(o, way, to).start(), way)
+                    my_copy(o, f).start()
+
+                side(d, s == d, masked_arrived)
 
         for d in range(R - 1, 0, -1):
             k = s - d - 1
@@ -301,16 +308,24 @@
                 for side in (from_left, from_right):
                     side(d, True, lambda o: my_copy(o, other_f).wait_recv())
 
-        done = s - R - 1 + 0
+            one_copy.wait()
+            two_copy.wait()
+
+        done = s - R - 1
 
         @pl.when(done >= 0)
         def _():
             c_copy(done, 0, sib).wait_recv()
             c_copy(done, 1, 3 - t).wait_recv()
-            product = lax.dot_general(
+            product[...] = lax.dot_general(
                 G[done], M[...], (((0,), (0,)), ((), ())), preferred_element_type=jnp.float32
             )
-            grad_out[pl.ds(pl.multiple_of(done * width, width), width), :] = product.astype(jnp.bfloat16)
+
+            @pl.loop(0, width // 32)
+            def _(i):
+                at = pl.ds(pl.multiple_of(done * width + i * 32, 32), 32)
+                grad = product[pl.ds(pl.multiple_of(i * 32, 32), 32), :] / float(2 * R * T)
+                W[at, :], one[at, :], two[at, :] = adamw(grad, W[at, :], one[at, :], two[at, :])
 
     ig_x_own.wait_recv()
 
@@ -351,34 +366,44 @@
     ig_x_own.wait_send()
 
 
+def write_out(*refs):
+    sem = refs[-1]
+    half = refs[0].shape[0] // 2
+    copies = [
+        pltpu.make_async_copy(
+            refs[i].at[pl.ds(j * half, half)], refs[3 + i].at[pl.ds(j * half, half)], sem.at[i, j]
+        )
+        for i in range(3) for j in range(2)
+    ]
+    for copy in copies:
+        copy.start()
+    for copy in copies:
+        copy.wait()
+
+
 def local_fast(R, activations, value_grads, lengths, master, moment_one, moment_two):
     T, D = activations.shape
     H, V = master.shape
     K = H // (4 * LANE)
     half = H // 2
     dma = pltpu.SemaphoreType.DMA
-    input_grads, grad_sum = pl.pallas_call(
+    input_grads, *state = pl.pallas_call(
         functools.partial(exchange, R, T, H, K),
         out_shape=(
             jax.ShapeDtypeStruct((T, half), jnp.bfloat16),
-            jax.ShapeDtypeStruct((H, V), jnp.bfloat16),
-        ),
-        in_specs=[
-            pl.BlockSpec(memory_space=pltpu.SMEM),
-            pl.BlockSpec(memory_space=pl.ANY),
-            pl.BlockSpec(memory_space=pltpu.VMEM),
-            pl.BlockSpec(memory_space=pl.ANY),
-        ],
-        out_specs=(pl.BlockSpec(memory_space=pltpu.VMEM), pl.BlockSpec(memory_space=pltpu.VMEM)),
+        ) + (jax.ShapeDtypeStruct((H, V), jnp.float32),) * 3,
+        in_specs=[pl.BlockSpec(memory_space=pltpu.SMEM)] + [pl.BlockSpec(memory_space=pl.ANY)] * 5,
+        out_specs=(pl.BlockSpec(memory_space=pltpu.VMEM),) * 4,
         scratch_shapes=[
             pltpu.VMEM((K, 2 * R * T, 4 * LANE), jnp.bfloat16),
             pltpu.VMEM((2 * R * T, V), jnp.bfloat16),
-            pltpu.VMEM((H, V), jnp.float32),
+            pltpu.VMEM((T, V), jnp.bfloat16),
+            pltpu.VMEM((4 * LANE, V), jnp.float32),
             pltpu.VMEM((2, 2 * T, half), jnp.bfloat16),
             pltpu.VMEM((2 * T, half), jnp.bfloat16),
             pltpu.VMEM((T, half), jnp.bfloat16),
             pltpu.VMEM((T, half), jnp.bfloat16),
-            dma((K, 2)), dma((2,)),
+            dma((K, 2)), dma((5,)),
             dma((K, 2)), dma((K, 2)),
             dma((K, R, 2)), dma((K, R)),
             dma((K, R)), dma((K, R)),
@@ -388,17 +413,21 @@
             dma((3,)), dma((3,)),
         ],
         compiler_params=pltpu.CompilerParams(
-            collective_id=0, has_side_effects=True, vmem_limit_bytes=32 * 1024 * 1024
+            collective_id=0, has_side_effects=True, vmem_limit_bytes=20 * 1024 * 1024
         ),
         cost_estimate=pl.CostEstimate(
-            flops=2 * 2 * R * T * H * V, bytes_accessed=20 * 1024 * 1024, transcendentals=0
+            flops=2 * 2 * R * T * H * V, bytes_accessed=60 * 1024 * 1024, transcendentals=0
         ),
-    )(lengths, activations, value_grads, master)
-    count = float(T * lax.axis_size("replica") * lax.axis_size("fsdp"))
-    new_master, new_one, new_two = adamw(
-        grad_sum.astype(jnp.float32) / count, master, moment_one, moment_two
-    )
-    return (input_grads, new_master, new_one, new_two)
+    )(lengths, activations, value_grads, master, moment_one, moment_two)
+    state = pl.pallas_call(
+        write_out,
+        out_shape=(jax.ShapeDtypeStruct((H, V), jnp.float32),) * 3,
+        in_specs=[pl.BlockSpec(memory_space=pltpu.VMEM)] * 3,
+        out_specs=(pl.BlockSpec(memory_space=pl.ANY),) * 3,
+        scratch_shapes=[dma((3, 2))],
+        compiler_params=pltpu.CompilerParams(vmem_limit_bytes=26 * 1024 * 1024),
+    )(*state)
+    return (input_grads, *state)
 
 
 def solution(mesh):

time: 111 us -> 96.7 us (0.87)
  the two profiles are of different devices: /device:TPU:1 before, /device:TPU:2 now
where the time goes in v2:
time: 96.7 us; the launch traced here: 95.7 us
  Pallas kernels  91.1 us (94%)
  local copies, waits for them, and re-layouts  3.94 us (4%)
    pallas_call x1, Pallas kernels, local_fast(): pl.pallas_call(functools.partial(exchange, R, T, H, K), out_shape=(jax.Sh...  82.6 us
    pallas_call x1, Pallas kernels, local_fast(): pl.pallas_call(write_out, out_shape=(jax.ShapeDtypeStruct((H, V), jnp.flo...  8.49 us
    unnamed x7, local copies, waits for them, and re-layouts  3.94 us

profile of v2, /device:TPU:2, one launch (start us, length us, event | category | flops | bytes accessed | tf_op | source)
XLA Modules:
  0.0 95.7 jit_solution(16498294109153309845)
XLA Ops:
  0.6 0.0 copy-start
  0.6 1.6 %copy-done = bf16[128,8192]{1,0:T(8,128)(2,1)S(1)} copy-done((bf16[128,8192]{1,0:T(8,128)(2,1)S(1)}, bf16[128,8192]{1,0:T(8,128)(2,1)}, u32[]{:S(2)}) %copy-start) | copy-done | bytes 2097176
  2.2 0.0 copy-start.1
  2.2 0.9 copy-done.1
  3.1 0.0 copy-start.2
  3.1 0.7 copy-done.2
  3.8 82.6 %shard_map.93 = (bf16[128,2048]{1,0:T(8,128)(2,1)S(1)}, f32[4096,512]{1,0:T(8,128)S(1)}, f32[4096,512]{1,0:T(8,128)S(1)}, f32[4096,512]{1,0:T(8,128)S(1)}) custom-call(s32[2]{0:T(128)S(1)} %copy-done.2, bf16[128,8192]{1,0:T(8,128)(2,1)S(1)} %copy-done, bf16[128,512]{1,0:T(8,128)(2,1)S(1)} %copy-done.1, f32[4096,512]{1,0:T(8,128)} %master.1, ...), custom_call_target="tpu_custom_call" | custom-call | flops 4294967296 | bytes 62914560 | tf_op jit(solution)/shard_map/pallas_call | solution.py:390
  86.4 8.5 %shard_map.94 = (f32[4096,512]{1,0:T(8,128)}, f32[4096,512]{1,0:T(8,128)}, f32[4096,512]{1,0:T(8,128)}) custom-call(f32[4096,512]{1,0:T(8,128)S(1)} %get-tuple-element.12.refs_0_, f32[4096,512]{1,0:T(8,128)S(1)} %get-tuple-element.13.refs_1_, f32[4096,512]{1,0:T(8,128)S(1)} %get-tuple-element.14.refs_2_), custom_call_target="tpu_custom_call" | custom-call | tf_op jit(solution)/shard_map/pallas_call | solution.py:422
  94.9 0.8 copy.11
Async XLA Ops:
  0.6 1.6 %copy-start = (bf16[128,8192]{1,0:T(8,128)(2,1)S(1)}, bf16[128,8192]{1,0:T(8,128)(2,1)}, u32[]{:S(2)}) copy-start(bf16[128,8192]{1,0:T(8,128)(2,1)} %acts.1) | copy-start | bytes 6291460
  2.2 0.9 copy-start.1
  3.1 0.7 copy-start.2

commit v3 on v2

--- a/solution.py
+++ b/solution.py
@@ -8,7 +8,7 @@
 from jax.sharding import PartitionSpec as P
 
 MESH = pl.DeviceIdType.MESH
-LANE = 128
+LANE = 256
 
 beta_one = 0.9
 beta_two = 0.95
@@ -241,8 +241,8 @@
             for side, way in ((from_left, 0), (from_right, 1)):
                 def arrived(o, k=k, way=way):
                     z_copy(k, o, way, o).wait_recv()
+                    x_copy(k, o, t).start()
                     pass_on(lambda to: z_copy(k, o, way, to).start(), way)
-                    x_copy(k, o, t).start()
 
                 side(d, jnp.logical_and(k >= 0, k < K), arrived)
 

time: 96.7 us -> 94.4 us (0.976)
  Pallas kernels: 91.1 us -> 89.7 us
    pallas_call x1, Pallas kernels: 82.6 us -> 81.2 us  [local_fast(): pl.pallas_call(functools.partial(exchange, R, T, H, K), out_shape=(jax.Sh...]
where the time goes in v3:
time: 94.4 us; the launch traced here: 94.3 us
  Pallas kernels  89.7 us (95%)
  local copies, waits for them, and re-layouts  3.94 us (4%)
    pallas_call x1, Pallas kernels, local_fast(): pl.pallas_call(functools.partial(exchange, R, T, H, K), out_shape=(jax.Sh...  81.2 us
    pallas_call x1, Pallas kernels, local_fast(): pl.pallas_call(write_out, out_shape=(jax.ShapeDtypeStruct((H, V), jnp.flo...  8.49 us
    unnamed x7, local copies, waits for them, and re-layouts  3.94 us

profile of v3, /device:TPU:2, one launch (start us, length us, event | category | flops | bytes accessed | tf_op | source)
XLA Modules:
  0.0 94.3 jit_solution(6788370437924545795)
XLA Ops:
  0.6 0.0 copy-start
  0.6 1.6 %copy-done = bf16[128,8192]{1,0:T(8,128)(2,1)S(1)} copy-done((bf16[128,8192]{1,0:T(8,128)(2,1)S(1)}, bf16[128,8192]{1,0:T(8,128)(2,1)}, u32[]{:S(2)}) %copy-start) | copy-done | bytes 2097176
  2.2 0.0 copy-start.1
  2.2 0.9 copy-done.1
  3.1 0.0 copy-start.2
  3.1 0.7 copy-done.2
  3.8 81.2 %shard_map.93 = (bf16[128,2048]{1,0:T(8,128)(2,1)S(1)}, f32[4096,512]{1,0:T(8,128)S(1)}, f32[4096,512]{1,0:T(8,128)S(1)}, f32[4096,512]{1,0:T(8,128)S(1)}) custom-call(s32[2]{0:T(128)S(1)} %copy-done.2, bf16[128,8192]{1,0:T(8,128)(2,1)S(1)} %copy-done, bf16[128,512]{1,0:T(8,128)(2,1)S(1)} %copy-done.1, f32[4096,512]{1,0:T(8,128)} %master.1, ...), custom_call_target="tpu_custom_call" | custom-call | flops 4294967296 | bytes 62914560 | tf_op jit(solution)/shard_map/pallas_call | solution.py:390
  85.0 8.5 %shard_map.94 = (f32[4096,512]{1,0:T(8,128)}, f32[4096,512]{1,0:T(8,128)}, f32[4096,512]{1,0:T(8,128)}) custom-call(f32[4096,512]{1,0:T(8,128)S(1)} %get-tuple-element.12.refs_0_, f32[4096,512]{1,0:T(8,128)S(1)} %get-tuple-element.13.refs_1_, f32[4096,512]{1,0:T(8,128)S(1)} %get-tuple-element.14.refs_2_), custom_call_target="tpu_custom_call" | custom-call | tf_op jit(solution)/shard_map/pallas_call | solution.py:422
  93.5 0.8 copy.11
Async XLA Ops:
  0.6 1.6 %copy-start = (bf16[128,8192]{1,0:T(8,128)(2,1)S(1)}, bf16[128,8192]{1,0:T(8,128)(2,1)}, u32[]{:S(2)}) copy-start(bf16[128,8192]{1,0:T(8,128)(2,1)} %acts.1) | copy-start | bytes 6291460
  2.2 0.9 copy-start.1
  3.1 0.7 copy-start.2

commit v4 on v3

--- a/solution.py
+++ b/solution.py
@@ -236,7 +236,7 @@
                 ).wait_recv()
             for way in (0, 1):
                 pass_on(lambda to, way=way: z_copy(s, r, way, to).start(), way)
-        for d in range(R - 1, 0, -1):
+        for d in range(1, R):
             k = s - d
             for side, way in ((from_left, 0), (from_right, 1)):
                 def arrived(o, k=k, way=way):
@@ -253,7 +253,7 @@
 
                 side(d, s == d, masked_arrived)
 
-        for d in range(R - 1, 0, -1):
+        for d in range(1, R):
             k = s - d - 1
             for side in (from_left, from_right):
                 side(d, jnp.logical_and(k >= 0, k < K),
@@ -368,13 +368,12 @@
 
 def write_out(*refs):
     sem = refs[-1]
-    half = refs[0].shape[0] // 2
-    copies = [
-        pltpu.make_async_copy(
-            refs[i].at[pl.ds(j * half, half)], refs[3 + i].at[pl.ds(j * half, half)], sem.at[i, j]
-        )
-        for i in range(3) for j in range(2)
-    ]
+    copies = []
+    for i in range(4):
+        half = refs[i].shape[0] // 2
+        for j in range(2):
+            at = pl.ds(j * half, half)
+            copies.append(pltpu.make_async_copy(refs[i].at[at], refs[4 + i].at[at], sem.at[i, j]))
     for copy in copies:
         copy.start()
     for copy in copies:
@@ -387,7 +386,7 @@
     K = H // (4 * LANE)
     half = H // 2
     dma = pltpu.SemaphoreType.DMA
-    input_grads, *state = pl.pallas_call(
+    results = pl.pallas_call(
         functools.partial(exchange, R, T, H, K),
         out_shape=(
             jax.ShapeDtypeStruct((T, half), jnp.bfloat16),
@@ -419,15 +418,14 @@
             flops=2 * 2 * R * T * H * V, bytes_accessed=60 * 1024 * 1024, transcendentals=0
         ),
     )(lengths, activations, value_grads, master, moment_one, moment_two)
-    state = pl.pallas_call(
+    return pl.pallas_call(
         write_out,
-        out_shape=(jax.ShapeDtypeStruct((H, V), jnp.float32),) * 3,
-        in_specs=[pl.BlockSpec(memory_space=pltpu.VMEM)] * 3,
-        out_specs=(pl.BlockSpec(memory_space=pl.ANY),) * 3,
-        scratch_shapes=[dma((3, 2))],
+        out_shape=tuple(jax.ShapeDtypeStruct(v.shape, v.dtype) for v in results),
+        in_specs=[pl.BlockSpec(memory_space=pltpu.VMEM)] * 4,
+        out_specs=(pl.BlockSpec(memory_space=pl.ANY),) * 4,
+        scratch_shapes=[dma((4, 2))],
         compiler_params=pltpu.CompilerParams(vmem_limit_bytes=26 * 1024 * 1024),
-    )(*state)
-    return (input_grads, *state)
+    )(*results)
 
 
 def solution(mesh):

time: 94.4 us -> 91 us (0.964)
  Pallas kernels: 89.7 us -> 87 us
    pallas_call x1, Pallas kernels: 81.2 us -> 78.4 us  [local_fast(): pl.pallas_call(functools.partial(exchange, R, T, H, K), out_shape=(jax.Sh...]
    unnamed x7 -> x6, local copies, waits for them, and re-layouts: 3.94 us -> 3.14 us
where the time goes in v4:
time: 91 us; the launch traced here: 90.8 us
  Pallas kernels  87 us (96%)
  local copies, waits for them, and re-layouts  3.14 us (3%)
    pallas_call x1, Pallas kernels, local_fast(): pl.pallas_call(functools.partial(exchange, R, T, H, K), out_shape=(jax.Sh...  78.4 us
    pallas_call x1, Pallas kernels, local_fast(): pl.pallas_call(write_out, out_shape=tuple((jax.ShapeDtypeStruct(v.shape,...  8.68 us
    unnamed x6, local copies, waits for them, and re-layouts  3.14 us

profile of v4, /device:TPU:2, one launch (start us, length us, event | category | flops | bytes accessed | tf_op | source)
XLA Modules:
  0.0 90.8 jit_solution(14603312188264469070)
XLA Ops:
  0.6 0.0 copy-start
  0.6 1.6 %copy-done = bf16[128,8192]{1,0:T(8,128)(2,1)S(1)} copy-done((bf16[128,8192]{1,0:T(8,128)(2,1)S(1)}, bf16[128,8192]{1,0:T(8,128)(2,1)}, u32[]{:S(2)}) %copy-start) | copy-done | bytes 2097176
  2.2 0.0 copy-start.1
  2.2 0.9 copy-done.1
  3.1 0.0 copy-start.2
  3.1 0.7 copy-done.2
  3.8 78.4 %shard_map.93 = (bf16[128,2048]{1,0:T(8,128)(2,1)S(1)}, f32[4096,512]{1,0:T(8,128)S(1)}, f32[4096,512]{1,0:T(8,128)S(1)}, f32[4096,512]{1,0:T(8,128)S(1)}) custom-call(s32[2]{0:T(128)S(1)} %copy-done.2, bf16[128,8192]{1,0:T(8,128)(2,1)S(1)} %copy-done, bf16[128,512]{1,0:T(8,128)(2,1)S(1)} %copy-done.1, f32[4096,512]{1,0:T(8,128)} %master.1, ...), custom_call_target="tpu_custom_call" | custom-call | flops 4294967296 | bytes 62914560 | tf_op jit(solution)/shard_map/pallas_call | solution.py:389
  82.2 8.7 %shard_map.94 = (bf16[128,2048]{1,0:T(8,128)(2,1)}, f32[4096,512]{1,0:T(8,128)}, f32[4096,512]{1,0:T(8,128)}, f32[4096,512]{1,0:T(8,128)}) custom-call(bf16[128,2048]{1,0:T(8,128)(2,1)S(1)} %get-tuple-element.8.refs_0_, f32[4096,512]{1,0:T(8,128)S(1)} %get-tuple-element.9.refs_1_, f32[4096,512]{1,0:T(8,128)S(1)} %get-tuple-element.10.refs_2_, ...), custom_call_target="tpu_custom_call" | custom-call | tf_op jit(solution)/shard_map/pallas_call | solution.py:421
Async XLA Ops:
  0.6 1.6 %copy-start = (bf16[128,8192]{1,0:T(8,128)(2,1)S(1)}, bf16[128,8192]{1,0:T(8,128)(2,1)}, u32[]{:S(2)}) copy-start(bf16[128,8192]{1,0:T(8,128)(2,1)} %acts.1) | copy-start | bytes 6291460
  2.2 0.9 copy-start.1
  3.1 0.7 copy-start.2
